TPU v7x, 256 devices: a whole 4x4x8 slice. The times are simulated.
256 devices in a mesh: group: 8 (over y_lo, x), blk: 32 (over y_hi, z, core).
Axes of the slice: x: 4, y: 4 (y_hi: 2, y_lo: 2; y = y_hi * 2 + y_lo), z: 8, core: 2. Of those that a mesh axis runs over, the one named last changes fastest.
Arguments:
- embeddings: bfloat16 [49152, 1024], P(('group', 'blk')), may hold values from -8 to 8
- block_cluster: int32 [3072], P(('group', 'blk')), may hold values from 0 to 24575, as said below
Outputs:
- best_match: float32 [49152], P(('group', 'blk'))
Inputs may be any that keep to these rules, and one draw needn't show every extreme that they name: `block_cluster`: among the 12 blocks of one device at most 3 have cluster ids of one remainder modulo 8. Every cluster has at most 128 blocks.
All inputs are finite; a program needn't handle non-finite values.
Results may differ from a plain program's by a relative error of at most 0.00055.
Values may be sent and summed in bfloat16 or wider, within the bound.
A program may use at most 64 MiB of HBM per device.

v0:
```python
import jax
import jax.numpy as jnp
from jax import lax
from jax.sharding import PartitionSpec as P

CAP = 3


def per_device(embeddings, block_cluster):
    helper_count = lax.axis_size("group")
    blocks_here = block_cluster.shape[0]
    rows_here = embeddings.shape[0]
    block_rows = rows_here // blocks_here
    feature_count = embeddings.shape[1]
    as_float = embeddings.astype(jnp.float32)
    normed = (
        as_float * lax.rsqrt(jnp.sum(as_float * as_float, axis=1, keepdims=True) + 1e-06)
    ).astype(jnp.bfloat16)
    target = block_cluster % helper_count
    same_target = target[:, None] == target[None, :]
    earlier = jnp.arange(blocks_here)[:, None] > jnp.arange(blocks_here)[None, :]
    rank_within = jnp.sum((same_target & earlier).astype(jnp.int32), axis=1)
    slot_of = target * CAP + rank_within
    slot_count = helper_count * CAP
    matches = slot_of[None, :] == jnp.arange(slot_count)[:, None]
    source = jnp.sum(
        matches.astype(jnp.int32) * jnp.arange(blocks_here, dtype=jnp.int32)[None, :], axis=1
    )
    filled = jnp.any(matches, axis=1)
    blocks = normed.reshape(blocks_here, block_rows, feature_count)
    outgoing = jnp.where(filled[:, None, None], blocks[source], jnp.zeros((), jnp.bfloat16))
    outgoing = outgoing.reshape(slot_count * block_rows, feature_count)
    outgoing_ids = jnp.repeat(jnp.where(filled, block_cluster[source], -1), block_rows)
    local_rows, local_ids = (
        lax.all_to_all(outgoing, "group", split_axis=0, concat_axis=0, tiled=True),
        lax.all_to_all(outgoing_ids, "group", split_axis=0, concat_axis=0, tiled=True),
    )
    slot_rows = local_rows.shape[0]
    position = lax.axis_index("blk") * slot_rows + jnp.arange(slot_rows, dtype=jnp.int32)
    visiting = lax.all_gather(local_rows, "blk", axis=0, tiled=True)
    visiting_ids = lax.all_gather(local_ids, "blk", axis=0, tiled=True)
    scores = lax.dot_general(
        local_rows, visiting, (((1,), (1,)), ((), ())), preferred_element_type=jnp.float32
    )
    others = jnp.arange(visiting.shape[0], dtype=jnp.int32)
    allowed = (local_ids[:, None] == visiting_ids[None, :]) & (position[:, None] != others[None, :])
    best = jnp.max(jnp.where(allowed, scores, -jnp.inf), axis=1)
    returned_max = lax.all_to_all(best, "group", split_axis=0, concat_axis=0, tiled=True)
    per_slot = returned_max.reshape(slot_count, block_rows)
    return per_slot[slot_of].reshape(rows_here)


def solution(mesh):
    in_specs = (P(("group", "blk"), None), P(("group", "blk")))
    out_specs = P(("group", "blk"))
    return jax.shard_map(
        per_device, mesh=mesh, in_specs=in_specs, out_specs=out_specs, check_vma=False
    )
```

profile of v0, /device:TPU:1, one launch (start us, length us, event | category | flops | bytes accessed | tf_op | source)
XLA Modules:
  0.0 248.3 jit_solution(16816175122741021192)
XLA Ops:
  6.5 0.0 all-gather.3.cloned.1.call-start
  6.5 0.7 and_select_fusion
  7.2 0.2 convert_reduce_fusion
  7.4 0.7 compare_select_fusion
  8.1 0.1 select_reduce_fusion.1
  8.1 0.1 fusion.3
  8.3 1.2 fusion.1
  9.4 1.1 fusion.2
  10.6 0.1 reduce_or.12
  10.6 0.1 broadcast_in_dim.50
  10.7 0.1 broadcast_in_dim.51
  10.8 0.6 gather_fusion.1
  11.4 0.1 bitcast_select_fusion
  11.6 17.7 %all_to_all.24 = bf16[8,48,1024]{2,1,0:T(8,128)(2,1)} all-to-all(bf16[8,48,1024]{2,1,0:T(8,128)(2,1)S(1)} %bitcast_select_fusion), channel_id=1, replica_groups=mesh['group'=8,'blk'=32] {'group'}, dimensions={0} | all-to-all | bytes 1572864 | tf_op jit(solution)/shard_map/all_to_all | solution.py:35
  29.3 0.0 all-gather.3.cloned.1.call-update
  29.3 1.4 gather_fusion
  30.7 0.1 gather.14
  30.8 0.1 broadcast_in_dim.48
  30.8 0.7 broadcast_in_dim.49
  31.5 3.3 %all-to-all-start = ((s32[8,48,1]{1,2,0:T(1,128)}), s32[8,48,1]{1,2,0:T(1,128)S(1)}, u32[]{:S(2)}, u32[]{:S(2)}) async-start(s32[8,48,1]{1,2,0:T(1,128)} %bitcast.2), calls=%async_computation | async-start | bytes 8192 | tf_op jit(solution)/shard_map/all_to_all | solution.py:36
  34.8 4.9 %all-to-all-done = s32[8,48,1]{1,2,0:T(1,128)S(1)} async-done(((s32[8,48,1]{1,2,0:T(1,128)}), s32[8,48,1]{1,2,0:T(1,128)S(1)}, u32[]{:S(2)}, u32[]{:S(2)}) %all-to-all-start) | async-done | bytes 1568 | tf_op jit(solution)/shard_map/all_to_all | solution.py:36
  39.8 0.1 reshape.93
  39.8 0.5 broadcast.91
  40.4 0.7 reduce.8
  41.0 0.1 eq.49
  41.1 47.5 %all-gather = s32[32,1,384]{2,1,0:T(1,128)S(1)} all-gather(s32[1,1,384]{2,1,0:T(1,128)S(1)} %reshape.93), channel_id=1, replica_groups=mesh['group'=8,'blk'=32] {'blk'}, dimensions={0}, use_global_device_ids=true | all-gather | bytes 50688 | tf_op jit(solution)/shard_map/all_gather | solution.py:41
  88.6 124.3 %all-gather.3.cloned.1.call-done = bf16[12288,1024]{1,0:T(8,128)(2,1)} async-done(((bf16[384,1024]{1,0:T(8,128)(2,1)}), bf16[12288,1024]{1,0:T(8,128)(2,1)}) %all-gather.3.cloned.1.call-update) | async-done | bytes 25165840 | tf_op jit(solution)/shard_map/all_gather | solution.py:40
  212.8 16.4 %select_reduce_fusion = f32[384]{0:T(512)S(1)} fusion(bf16[384,1024]{1,0:T(8,128)(2,1)} %bitcast.18, bf16[12288,1024]{1,0:T(8,128)(2,1)} %all-gather.3.cloned.1.call-done, s32[384]{0:T(512)S(1)} %iota_add_fusion, s32[12288]{0:T(1024)S(1)} %bitcast.20, s32[384]{0:T(512)S(1)} %eq.49), kind=kOutput, calls=%fused_computation.3 | convolution fusion | flops 9687269376 | bytes 26006016 | tf_op jit(solution)/shard_map/dot_general | solution.py:42
  229.3 0.7 all_to_all.19
  230.0 4.0 %all-to-all-start.2 = ((f32[8,48,1]{1,2,0:T(1,128)}), f32[8,48,1]{1,2,0:T(1,128)S(1)}, u32[]{:S(2)}, u32[]{:S(2)}) async-start(f32[8,48,1]{1,2,0:T(1,128)} %all_to_all.19), calls=%async_computation.2 | async-start | bytes 8192 | tf_op jit(solution)/shard_map/all_to_all | solution.py:48
  234.0 5.0 %all-to-all-done.2 = f32[8,48,1]{1,2,0:T(1,128)S(1)} async-done(((f32[8,48,1]{1,2,0:T(1,128)}), f32[8,48,1]{1,2,0:T(1,128)S(1)}, u32[]{:S(2)}, u32[]{:S(2)}) %all-to-all-start.2) | async-done | bytes 1568 | tf_op jit(solution)/shard_map/all_to_all | solution.py:48
  239.0 0.5 broadcast.92
  239.5 0.7 reduce.9
  240.2 0.1 reshape.66
  240.2 0.6 gather_fusion.2
  240.8 0.6 reshape.67
  (6 shorter events, 0.0 us)
Async XLA Ops:
  6.5 206.3 %all-gather.3.cloned.1.call-start = ((), (), s32[]{:S(2)}) async-start(), calls=%async_computation.3 | async-start | bytes 25952256 | tf_op jit(solution)/shard_map/all_gather | solution.py:40
  31.5 8.2 %all-to-all-start = ((s32[8,48,1]{1,2,0:T(1,128)}), s32[8,48,1]{1,2,0:T(1,128)S(1)}, u32[]{:S(2)}, u32[]{:S(2)}) async-start(s32[8,48,1]{1,2,0:T(1,128)} %bitcast.2), calls=%async_computation | async-start | bytes 8192 | tf_op jit(solution)/shard_map/all_to_all | solution.py:36
  230.0 9.0 %all-to-all-start.2 = ((f32[8,48,1]{1,2,0:T(1,128)}), f32[8,48,1]{1,2,0:T(1,128)S(1)}, u32[]{:S(2)}, u32[]{:S(2)}) async-start(f32[8,48,1]{1,2,0:T(1,128)} %all_to_all.19), calls=%async_computation.2 | async-start | bytes 8192 | tf_op jit(solution)/shard_map/all_to_all | solution.py:48
Sparse Core Ops, SparseCore 0:
  29.4 183.3 all-gather.2
where the time goes:
time: 249 us; the launch traced here: 248 us
  waiting for transfers between devices  134 us (54%)
  blocking collectives  65.2 us (26%)
  matrix products  16.4 us (7%)
  between operations  13.5 us (5%)
  starting transfers between devices  7.29 us (3%)
  local copies, waits for them, and re-layouts  6.2 us (2%)
  other arithmetic  5.46 us (2%)
    all_gather x1, waiting for transfers between devices, per_device(): visiting = lax.all_gather(local_rows, 'blk', axis=0, tiled=True)  124 us
    all_gather x1, blocking collectives, per_device(): visiting_ids = lax.all_gather(local_ids, 'blk', axis=0, tiled=True)  47.5 us
    all_to_all x1, blocking collectives, per_device(): lax.all_to_all(outgoing, 'group', split_axis=0, concat_axis=0, tiled=True)  17.7 us
    dot_general x1, matrix products, per_device(): lax.dot_general(local_rows, visiting, (((1,), (1,)), ((), ())), preferred...  16.4 us
    all_to_all x1, waiting for transfers between devices, per_device(): lax.all_to_all(best, 'group', split_axis=0, concat_axis=0, tiled=True)  4.99 us
  transfers between devices with their start and end apart: 3, of which 3 were waited for; matrix products, arithmetic and copies ran while one was open for 1% of the time, Pallas kernels for 0%

commit v1 on v0

v1 whole, which is shorter than its diff:
```python
import jax
import jax.numpy as jnp
from jax import lax
from jax.experimental import pallas as pl
from jax.experimental.pallas import tpu as pltpu
from jax.sharding import PartitionSpec as P

MESH = pl.DeviceIdType.MESH
SIZES = (4, 4, 8)
ROWS = 192
CHIP = 2 * ROWS
BLOCK = 16
BLOCKS = ROWS // BLOCK
WIDTH = 1024
LANES = 128
NEG = float("-inf")
NT = (((1,), (1,)), ((), ()))

OFFSETS = (
    (0, 0, 0),
    (0, 1, 7),
    (0, 0, 7),
    (0, 1, 0),
    (1, 3, 0),
    (2, 3, 0),
    (3, 3, 0),
    (0, 0, 1),
    (0, 0, 2),
    (1, 0, 2),
    (2, 0, 2),
    (3, 0, 2),
    (0, 1, 5),
    (0, 1, 6),
    (0, 2, 6),
    (0, 0, 6),
)
PARENTS = (
    (-1, 3, 1, 0, 5, 6, 0, 0, 7, 8, 9, 8, 13, 1, 13, 13),
    (-1, 13, 0, 0, 5, 6, 0, 0, 7, 8, 11, 8, 13, 15, 13, 2),
    (-1, 3, 1, 0, 0, 4, 5, 0, 7, 8, 11, 8, 13, 1, 13, 13),
    (-1, 2, 0, 0, 0, 4, 5, 0, 7, 8, 9, 8, 13, 15, 13, 2),
)
FIRST = (
    (0, 6), (0, 3), (0, 7), (1, 2), (2, 4), (1, 6), (2, 3), (1, 7),
    (3, 2), (3, 4), (1, 3), (2, 7), (3, 7), (3, 3),
)
PROGRAM = (
    (2, 1), (3, 0), (7, 0), (4, 2), (6, 0), (2, 3), (3, 2), (7, 1), (4, 3), (6, 1),
    (1, 0), (3, 1), (7, 2), (5, 0), (5, 2), (1, 3), (7, 3), (15, 1), (5, 1), (5, 3),
    (2, 0), (1, 2), (3, 3), (8, 0), (4, 0), (6, 2), (8, 1), (13, 1), (15, 3), (4, 1),
    (6, 3), (-1, 0), (2, 2), (8, 2), (13, 0), (9, 0), (11, 0), (-1, 1), (-1, 2), (14, 1),
    (8, 3), (13, 2), (9, 1), (11, 1), (-1, 3), (13, 3), (15, 0), (1, 1), (12, 0), (10, 0),
    (11, 2), (-1, 4), (14, 0), (15, 2), (12, 1), (9, 3), (10, 1), (-1, 5), (-1, 6), (14, 2),
    (12, 2), (9, 2), (10, 2), (-1, 7), (-1, 8), (14, 3), (12, 3), (10, 3), (11, 3), (-1, 9),
    (-1, 10), (-1, 11), (-1, 12), (-1, 13), (-1, 14), (-1, 15), (-1, 16),
)
STEPS = (
    ((0, 7, 0, 5), (5, 7, 0, 3),),
    ((3, 7, 3, 5), (0, 4, 0, 6),),
    ((4, 7, 6, 7), (4, 5, 3, 4),),
    ((4, 6, 2, 7), (2, 5, 2, 3),),
    ((2, 4, 2, 6), (5, 8, 3, 8),),
    ((4, 8, 6, 8), (2, 8, 7, 13),),
    ((5, 13, 4, 13), (6, 13, 8, 13),),
    ((1, 5, 1, 4), (1, 6, 5, 15),),
    ((3, 15, 4, 15), (6, 15, 8, 15),),
    ((0, 9, 7, 9), (2, 9, 9, 13),),
    ((1, 9, 9, 15), (0, 14, 7, 14),),
    ((2, 14, 8, 14), (14, 15, 9, 14),),
    ((5, 12, 4, 12), (6, 12, 8, 12),),
    ((9, 12, 0, 10), (0, 11, 7, 10),),
    ((7, 11, 2, 10), (2, 11, 10, 13),),
    ((11, 13, 1, 10), (1, 11, 10, 15),),
    ((10, 14, 10, 12), (11, 12, 10, 12),),
)

SLOTS = len(OFFSETS)
PARTS = len(PARENTS)
PART = ROWS // PARTS


def minus(a, b):
    return tuple((p - q) % m for p, q, m in zip(a, b, SIZES))


ORIGIN = (0, 0, 0)


def partners():
    found = {(ORIGIN, 1)}
    for offset in OFFSETS[1:]:
        for flip in (0, 1):
            found.add((offset, flip))
            found.add((minus(ORIGIN, offset), flip))
    for parents in PARENTS:
        for slot in range(1, SLOTS):
            hop = minus(OFFSETS[parents[slot]], OFFSETS[slot])
            found.add((hop, 0))
            found.add((minus(ORIGIN, hop), 0))
    return sorted(found)


def kernel(
    ids_ref, emb_ref, out_ref,
    buf, idb, idcol, idrow, racc, cacc, mat, res, rin,
    data_s, data_r, swap_s, swap_r, id_s, id_r, ret_s, ret_r,
):
    group = lax.axis_index("group")
    blk = lax.axis_index("blk")
    core = lax.rem(blk, 2)
    place = (lax.rem(group, 4), (blk // 16) * 2 + group // 4, lax.rem(blk // 2, 8))

    def device(offset, flip):
        x, y, z = (lax.rem(p + o, m) if o else p for p, o, m in zip(place, offset, SIZES))
        there = 1 - core if flip else core
        return (lax.rem(y, 2) * 4 + x, (y // 2) * 16 + z * 2 + there)

    barrier = pltpu.get_barrier_semaphore()
    everyone = partners()
    for offset, flip in everyone:
        pl.semaphore_signal(barrier, inc=1, device_id=device(offset, flip), device_id_type=MESH)

    def rows_of(slot, part, count):
        return pl.ds(pl.multiple_of(slot * CHIP + core * ROWS + part * PART, BLOCK), count)

    own = rows_of(0, 0, ROWS)
    as_float = emb_ref[...].astype(jnp.float32)
    total = jnp.sum(as_float * as_float, axis=1, keepdims=True)
    buf[own, :] = (as_float * lax.rsqrt(total + 1e-06)).astype(jnp.bfloat16)
    for block in range(BLOCKS):
        idb[0, core, pl.ds(block, 1), :] = jnp.full((1, LANES), ids_ref[block], jnp.int32)
    idb[0, core, pl.ds(BLOCKS, BLOCK - BLOCKS), :] = jnp.full((BLOCK - BLOCKS, LANES), -1, jnp.int32)
    pl.semaphore_wait(barrier, len(everyone))

    def id_copy(slot, flip):
        return pltpu.make_async_remote_copy(
            src_ref=idb.at[0, core], dst_ref=idb.at[slot, core], send_sem=id_s.at[slot, flip], recv_sem=id_r.at[slot, core],
            device_id=device(minus(ORIGIN, OFFSETS[slot]), flip), device_id_type=MESH)

    def data_copy(slot, part):
        parent = PARENTS[part][slot]
        return pltpu.make_async_remote_copy(
            src_ref=buf.at[rows_of(parent, part, PART), :], dst_ref=buf.at[rows_of(slot, part, PART), :],
            send_sem=data_s.at[slot, part], recv_sem=data_r.at[slot, part],
            device_id=device(minus(OFFSETS[parent], OFFSETS[slot]), 0), device_id_type=MESH)

    def swap_copy(slot):
        return pltpu.make_async_remote_copy(
            src_ref=buf.at[rows_of(slot, 0, ROWS), :], dst_ref=buf.at[rows_of(slot, 0, ROWS), :],
            send_sem=swap_s.at[slot], recv_sem=swap_r.at[slot], device_id=device(ORIGIN, 1), device_id_type=MESH)

    def return_copy(slot, flip):
        return pltpu.make_async_remote_copy(
            src_ref=res.at[pl.ds(slot, 1), :], dst_ref=rin.at[pl.ds(slot * 2 + core, 1), :],
            send_sem=ret_s.at[slot, flip], recv_sem=ret_r.at[slot, core],
            device_id=device(OFFSETS[slot], flip), device_id_type=MESH)

    fan = [(slot, flip) for slot in range(SLOTS) for flip in (0, 1) if (slot, flip) != (0, 0)]
    for slot, flip in fan:
        id_copy(slot, flip).start()
    for part, slot in FIRST:
        data_copy(slot, part).start()
    swap_copy(0).start()

    racc[...] = jnp.full(racc.shape, NEG, jnp.float32)
    cacc[...] = jnp.full(cacc.shape, NEG, jnp.float32)

    def wait_id(slot, sender):
        pltpu.make_async_remote_copy(
            src_ref=idb.at[0, core], dst_ref=idb.at[slot, sender], send_sem=id_s.at[slot, 0], recv_sem=id_r.at[slot, sender],
            device_id=device(ORIGIN, 1), device_id_type=MESH).wait_recv()

    wait_id(0, 1 - core)
    for slot in range(1, SLOTS):
        for sender in (0, 1):
            wait_id(slot, sender)

    lane = lax.broadcasted_iota(jnp.int32, (1, CHIP), 1)

    def prepare(slot, carry):
        row = jnp.zeros((1, CHIP), jnp.int32)
        for half in (0, 1):
            tile = idb[slot, half]
            for block in range(BLOCKS):
                splat = tile[block:block + 1, :]
                at = half * ROWS + block * BLOCK
                idcol[pl.ds(pl.multiple_of(slot * CHIP, CHIP) + at, BLOCK), :] = jnp.broadcast_to(splat, (BLOCK, LANES))
                row = jnp.where(lane // BLOCK == at // BLOCK, jnp.concatenate([splat] * 3, axis=1), row)
        idrow[pl.ds(pl.multiple_of(slot * 8, 8), 8), :] = jnp.broadcast_to(row, (8, CHIP))
        return carry

    lax.fori_loop(0, SLOTS, prepare, 0)

    def merge(first, second, count, itself):
        left = pl.ds(pl.multiple_of(first, BLOCK), count)
        right = pl.ds(pl.multiple_of(second * CHIP, CHIP), CHIP)
        top = pl.ds(pl.multiple_of(second * 8, 8), 8)
        scores = lax.dot_general(buf[left, :], buf[right, :], NT, preferred_element_type=jnp.float32)
        mine = idcol[left, :]
        theirs = idrow[pl.ds(pl.multiple_of(second * 8, 8), 1), :]
        best = racc[left, :]
        tops = []
        for tile in range(CHIP // LANES):
            cut = slice(tile * LANES, (tile + 1) * LANES)
            allowed = mine == theirs[:, cut]
            if itself:
                here = lax.broadcasted_iota(jnp.int32, (count, LANES), 0) + first
                there = lax.broadcasted_iota(jnp.int32, (count, LANES), 1) + tile * LANES
                allowed = allowed & (here != there)
            kept = jnp.where(allowed, scores[:, cut], NEG)
            best = jnp.maximum(best, kept)
            if not itself:
                tops.append(jnp.max(kept.reshape(count // 8, 8, LANES), axis=0))
        racc[left, :] = best
        if not itself:
            cacc[top, :] = jnp.maximum(cacc[top, :], jnp.concatenate(tops, axis=1))

    have = set()

    def need(slot):
        if slot not in have:
            have.add(slot)
            swap_copy(slot).wait_recv()

    need(0)
    merge(core * ROWS, 0, ROWS, True)

    arrived = [0] * SLOTS
    for slot, index in PROGRAM:
        if slot >= 0:
            data_copy(slot, index).wait_recv()
            for child in range(1, SLOTS):
                if PARENTS[index][child] == slot:
                    data_copy(child, index).start()
            arrived[slot] += 1
            if arrived[slot] == PARTS:
                swap_copy(slot).start()
        else:
            for one in STEPS[index]:
                for other in one:
                    need(other)
            for p0, q0, p1, q1 in STEPS[index]:
                merge((p0 + core * (p1 - p0)) * CHIP, q0 + core * (q1 - q0), CHIP, False)

    lanes = lax.broadcasted_iota(jnp.int32, (CHIP, LANES), 1)
    mat[...] = jnp.full(mat.shape, NEG, jnp.float32)

    def reduce(slot, carry):
        wide = racc[pl.ds(pl.multiple_of(slot * CHIP, CHIP), CHIP), :]
        mat[...] = jnp.where(lanes == slot, jnp.max(wide, axis=1, keepdims=True), mat[...])
        return carry

    lax.fori_loop(0, SLOTS, reduce, 0)
    turned = jnp.transpose(mat[...])[:SLOTS]
    res[...] = jnp.maximum(turned, jnp.max(cacc[...].reshape(SLOTS, 8, CHIP), axis=1))

    for slot, flip in reversed(fan):
        return_copy(slot, flip).start()
    rin[pl.ds(core, 1), :] = res[pl.ds(0, 1), :]

    def wait_return(slot, sender):
        pltpu.make_async_remote_copy(
            src_ref=res.at[pl.ds(slot, 1), :], dst_ref=rin.at[pl.ds(slot * 2 + sender, 1), :],
            send_sem=ret_s.at[slot, 0], recv_sem=ret_r.at[slot, sender],
            device_id=device(ORIGIN, 1), device_id_type=MESH).wait_recv()

    wait_return(0, 1 - core)
    for slot in range(1, SLOTS):
        for sender in (0, 1):
            wait_return(slot, sender)
    joined = jnp.max(rin[...], axis=0, keepdims=True)
    out_ref[...] = jnp.where(core == 0, joined[:, :ROWS], joined[:, ROWS:])

    for slot, flip in fan:
        id_copy(slot, flip).wait_send()
        return_copy(slot, flip).wait_send()
    swap_copy(0).wait_send()
    for slot in range(1, SLOTS):
        for part in range(PARTS):
            data_copy(slot, part).wait_send()
        swap_copy(slot).wait_send()


def per_device(embeddings, block_cluster):
    vmem = pl.BlockSpec(memory_space=pltpu.VMEM)
    dma = pltpu.SemaphoreType.DMA
    out = pl.pallas_call(
        kernel,
        out_shape=jax.ShapeDtypeStruct((1, ROWS), jnp.float32),
        in_specs=[pl.BlockSpec(memory_space=pltpu.SMEM), vmem],
        out_specs=vmem,
        scratch_shapes=[
            pltpu.VMEM((SLOTS * CHIP, WIDTH), jnp.bfloat16),
            pltpu.VMEM((SLOTS, 2, BLOCK, LANES), jnp.int32),
            pltpu.VMEM((SLOTS * CHIP, LANES), jnp.int32),
            pltpu.VMEM((SLOTS * 8, CHIP), jnp.int32),
            pltpu.VMEM((SLOTS * CHIP, LANES), jnp.float32),
            pltpu.VMEM((SLOTS * 8, CHIP), jnp.float32),
            pltpu.VMEM((CHIP, LANES), jnp.float32),
            pltpu.VMEM((SLOTS, CHIP), jnp.float32),
            pltpu.VMEM((SLOTS * 2, CHIP), jnp.float32),
            dma((SLOTS, PARTS)), dma((SLOTS, PARTS)),
            dma((SLOTS,)), dma((SLOTS,)),
            dma((SLOTS, 2)), dma((SLOTS, 2)),
            dma((SLOTS, 2)), dma((SLOTS, 2)),
        ],
        compiler_params=pltpu.CompilerParams(
            collective_id=0, has_side_effects=True, vmem_limit_bytes=40 * 2**20),
    )(block_cluster, embeddings)
    return out.reshape(ROWS)


def solution(mesh):
    return jax.shard_map(
        per_device, mesh=mesh, in_specs=(P(("group", "blk"), None), P(("group", "blk"))), out_specs=P(("group", "blk")),
        check_vma=False,
    )
```

time: 249 us -> 70.7 us (0.28)
  waiting for transfers between devices: 134 us -> 0 us
  Pallas kernels: 0 us -> 68.3 us
  blocking collectives: 65.2 us -> 0 us
  matrix products: 16.4 us -> 0 us
  between operations: 13.5 us -> 0.01 us
  starting transfers between devices: 7.29 us -> 0 us
  other arithmetic: 5.46 us -> 0 us
  local copies, waits for them, and re-layouts: 6.2 us -> 2.21 us
    all_gather x1 -> x0, waiting for transfers between devices: 124 us -> none  [per_device(): visiting = lax.all_gather(local_rows, 'blk', axis=0, tiled=True)]
    pallas_call x0 -> x1, Pallas kernels: none -> 68.3 us  [per_device(): pl.pallas_call(kernel, out_shape=jax.ShapeDtypeStruct((1, ROWS), jnp.floa...]
    all_gather x1 -> x0, blocking collectives: 47.5 us -> none  [per_device(): visiting_ids = lax.all_gather(local_ids, 'blk', axis=0, tiled=True)]
    all_to_all x1 -> x0, blocking collectives: 17.7 us -> none  [per_device(): lax.all_to_all(outgoing, 'group', split_axis=0, concat_axis=0, tiled=True)]
    dot_general x1 -> x0, matrix products: 16.4 us -> none  [per_device(): lax.dot_general(local_rows, visiting, (((1,), (1,)), ((), ())), preferred...]
    all_to_all x2 -> x0, waiting for transfers between devices: 9.91 us -> none  [the longest x1 4.99 us: per_device(): lax.all_to_all(best, 'group', split_axis=0, concat_axis=0, tiled=True)]
    all_to_all x2 -> x0, starting transfers between devices: 7.29 us -> none  [the longest x1 4 us: per_device(): lax.all_to_all(best, 'group', split_axis=0, concat_axis=0, tiled=True)]
    gather x4 -> x0, local copies, waits for them, and re-layouts: 2.6 us -> none  [the longest x2 1.43 us: per_device(): block_cluster[source]]
  transfers between devices with their start and end apart: 3 -> 0, of which waited for: 3 -> 0; matrix products, arithmetic and copies ran while one was open for 1% -> 0% of each run, Pallas kernels for 0% -> 0%
where the time goes in v1:
time: 70.7 us; the launch traced here: 70.5 us
  Pallas kernels  68.3 us (97%)
  local copies, waits for them, and re-layouts  2.21 us (3%)
    pallas_call x1, Pallas kernels, per_device(): pl.pallas_call(kernel, out_shape=jax.ShapeDtypeStruct((1, ROWS), jnp.floa...  68.3 us
    unnamed x5, local copies, waits for them, and re-layouts  2.21 us

profile of v1, /device:TPU:1, one launch (start us, length us, event | category | flops | bytes accessed | tf_op | source)
XLA Modules:
  0.0 70.5 jit_solution(5475920414090548356)
XLA Ops:
  0.0 0.0 copy-start
  0.0 1.0 %copy-done = bf16[192,1024]{1,0:T(8,128)(2,1)S(1)} copy-done((bf16[192,1024]{1,0:T(8,128)(2,1)S(1)}, bf16[192,1024]{1,0:T(8,128)(2,1)}, u32[]{:S(2)}) %copy-start) | copy-done | bytes 393240
  1.0 0.0 copy-start.1
  1.0 0.7 copy-done.1
  1.7 68.3 %shard_map.28 = f32[1,192]{1,0:T(1,128)S(1)} custom-call(s32[12]{0:T(128)S(1)} %copy-done.1, bf16[192,1024]{1,0:T(8,128)(2,1)S(1)} %copy-done), custom_call_target="tpu_custom_call" | custom-call | tf_op jit(solution)/shard_map/pallas_call | solution.py:287
  70.0 0.6 copy.4
Async XLA Ops:
  0.0 1.0 %copy-start = (bf16[192,1024]{1,0:T(8,128)(2,1)S(1)}, bf16[192,1024]{1,0:T(8,128)(2,1)}, u32[]{:S(2)}) copy-start(bf16[192,1024]{1,0:T(8,128)(2,1)} %emb_ref.1) | copy-start | bytes 1179652
  1.0 0.7 copy-start.1

commit v2 on v1

v2 whole, which is shorter than its diff:
```python
import jax
import jax.numpy as jnp
from jax import lax
from jax.experimental import pallas as pl
from jax.experimental.pallas import tpu as pltpu
from jax.sharding import PartitionSpec as P

MESH = pl.DeviceIdType.MESH
SIZES = (4, 4, 8)
ROWS = 192
CHIP = 2 * ROWS
BLOCK = 16
BLOCKS = ROWS // BLOCK
WIDTH = 1024
LANES = 128
NEG = float("-inf")
NT = (((1,), (1,)), ((), ()))

SEND, SWAP, STEP, FOLD = range(4)
OFFSETS = (
    (0, 0, 0), (0, 0, 7), (1, 0, 7), (2, 0, 7), (3, 0, 7), (2, 0, 0), (0, 1, 0), (3, 1, 0),
    (0, 2, 0), (0, 3, 0), (0, 0, 2), (0, 1, 2), (0, 2, 2), (0, 3, 2), (0, 0, 6), (1, 0, 6),
    (2, 0, 6),
)
PARENTS = (
    (-1, 0, 1, 2, 3, 3, 0, 6, 6, 0, 0, 12, 13, 10, 15, 16, 3),
    (-1, 0, 3, 5, 1, 0, 0, 6, 6, 0, 13, 10, 13, 9, 4, 2, 15),
    (-1, 0, 1, 5, 3, 0, 0, 6, 6, 0, 13, 10, 13, 9, 15, 2, 15),
    (-1, 0, 1, 2, 1, 3, 0, 6, 9, 0, 0, 10, 13, 10, 1, 2, 3),
)
PROGRAM = (
    (SEND, 1, 0), (SEND, 5, 1), (SEND, 6, 0), (SEND, 9, 0), (SEND, 10, 0), (SWAP, 0, 0), (SEND, 5, 2),
    (SEND, 1, 3), (SEND, 6, 3), (SEND, 9, 2), (SEND, 1, 2), (SEND, 6, 2), (SEND, 9, 3), (SEND, 10, 3),
    (SEND, 2, 0), (SEND, 7, 0), (SEND, 6, 1), (SEND, 9, 1), (SEND, 3, 1), (SEND, 2, 3), (SEND, 7, 3),
    (SEND, 8, 0), (SEND, 3, 2), (SEND, 13, 2), (SEND, 13, 0), (SEND, 2, 2), (SEND, 7, 2), (SEND, 1, 1),
    (SEND, 8, 2), (SEND, 8, 3), (SEND, 3, 0), (SWAP, 6, 0), (SWAP, 9, 0), (SEND, 7, 1), (SEND, 8, 1),
    (SEND, 13, 1), (SEND, 15, 3), (SEND, 13, 3), (SEND, 2, 1), (SEND, 3, 3), (SEND, 11, 3), (SEND, 12, 0),
    (SEND, 15, 2), (SEND, 4, 3), (SEND, 4, 2), (SWAP, 1, 0), (SWAP, 7, 0), (SEND, 10, 2), (SEND, 12, 2),
    (SEND, 16, 0), (SEND, 5, 0), (SEND, 4, 1), (SEND, 4, 0), (SWAP, 8, 0), (STEP, 0, 0), (SEND, 12, 3),
    (SWAP, 2, 0), (SEND, 15, 1), (SWAP, 3, 0), (SEND, 5, 3), (STEP, 1, 0), (SEND, 14, 2), (SEND, 16, 2),
    (SEND, 14, 3), (SEND, 11, 0), (SEND, 10, 1), (SWAP, 13, 0), (STEP, 2, 0), (STEP, 3, 0), (SEND, 15, 0),
    (SEND, 11, 2), (SEND, 14, 1), (SEND, 12, 1), (SWAP, 4, 0), (STEP, 4, 0), (SEND, 16, 1), (SWAP, 5, 0),
    (SEND, 16, 3), (STEP, 5, 0), (SEND, 11, 1), (SWAP, 10, 0), (STEP, 6, 0), (STEP, 7, 0), (SEND, 14, 0),
    (SWAP, 15, 0), (STEP, 8, 0), (SWAP, 12, 0), (STEP, 9, 0), (STEP, 10, 0), (STEP, 11, 0), (STEP, 12, 0),
    (STEP, 13, 0), (FOLD, 0, 0), (STEP, 14, 0), (STEP, 15, 0), (STEP, 16, 0), (STEP, 17, 0), (STEP, 18, 0),
    (STEP, 19, 0), (STEP, 20, 0),
)
STEPS = (
    ((6, 0, 6, 9), (1, 0, 1, 6),),
    ((1, 9, 7, 0), (7, 6, 7, 9),),
    ((7, 1, 8, 1), (8, 7, 2, 0),),
    ((2, 9, 2, 8), (3, 0, 3, 1),),
    ((3, 6, 3, 9), (3, 7, 3, 8),),
    ((13, 0, 13, 1), (13, 6, 13, 7),),
    ((13, 8, 13, 9), (13, 2, 13, 3),),
    ((4, 0, 4, 8), (4, 9, 4, 13),),
    ((5, 6, 5, 8), (5, 13, 10, 1),),
    ((10, 2, 10, 3), (10, 7, 10, 4),),
    ((10, 5, 15, 0), (15, 5, 15, 6),),
    ((15, 7, 15, 8), (15, 9, 15, 13),),
    ((15, 10, 12, 1), (12, 2, 12, 3),),
    ((12, 4, 12, 5),),
    ((12, 7), (12, 15),),
    ((11, 1), (11, 2),),
    ((11, 3), (11, 4),),
    ((11, 15), (16, 10),),
    ((16, 13), (16, 12),),
    ((14, 10), (14, 12),),
    ((14, 13),),
)

SLOTS = len(OFFSETS)
PARTS = len(PARENTS)
PART = ROWS // PARTS


def minus(a, b):
    return tuple((p - q) % m for p, q, m in zip(a, b, SIZES))


ORIGIN = (0, 0, 0)


def partners():
    found = {(ORIGIN, 1)}
    for parents in PARENTS:
        for slot in range(1, SLOTS):
            hop = minus(OFFSETS[parents[slot]], OFFSETS[slot])
            found.add((hop, 0))
            found.add((minus(ORIGIN, hop), 0))
    return sorted(found)


def kernel(
    ids_ref, emb_ref, out_ref,
    emb, ids, buf, idb, idcol, idrow, racc, cacc, mat, res, rin,
    load, data_s, data_r, swap_s, swap_r, id_s, id_r, ids_s, ids_r, ret_s, ret_r,
):
    loads = [pltpu.make_async_copy(emb_ref, emb, load.at[0]), pltpu.make_async_copy(ids_ref, ids, load.at[1])]
    for one in loads:
        one.start()
    group = lax.axis_index("group")
    blk = lax.axis_index("blk")
    core = lax.rem(blk, 2)
    place = (lax.rem(group, 4), (blk // 16) * 2 + group // 4, lax.rem(blk // 2, 8))

    def device(offset, flip):
        x, y, z = (lax.rem(p + o, m) if o else p for p, o, m in zip(place, offset, SIZES))
        there = 1 - core if flip else core
        return (lax.rem(y, 2) * 4 + x, (y // 2) * 16 + z * 2 + there)

    barrier = pltpu.get_barrier_semaphore()
    everyone = partners()
    for offset, flip in everyone:
        pl.semaphore_signal(barrier, inc=1, device_id=device(offset, flip), device_id_type=MESH)

    def rows_of(slot, part, count):
        return pl.ds(pl.multiple_of(slot * CHIP + core * ROWS + part * PART, BLOCK), count)

    own = rows_of(0, 0, ROWS)
    for one in loads:
        one.wait()
    as_float = emb[...].astype(jnp.float32)
    total = jnp.sum(as_float * as_float, axis=1, keepdims=True)
    buf[own, :] = (as_float * lax.rsqrt(total + 1e-06)).astype(jnp.bfloat16)
    for block in range(BLOCKS):
        idb[0, core, pl.ds(block, 1), :] = jnp.full((1, LANES), ids[block], jnp.int32)
    idb[0, core, pl.ds(BLOCKS, BLOCK - BLOCKS), :] = jnp.full((BLOCK - BLOCKS, LANES), -1, jnp.int32)
    pl.semaphore_wait(barrier, len(everyone))

    def data_copy(slot, part):
        parent = PARENTS[part][slot]
        return pltpu.make_async_remote_copy(
            src_ref=buf.at[rows_of(parent, part, PART), :], dst_ref=buf.at[rows_of(slot, part, PART), :],
            send_sem=data_s.at[slot, part], recv_sem=data_r.at[slot, part],
            device_id=device(minus(OFFSETS[parent], OFFSETS[slot]), 0), device_id_type=MESH)

    def id_copy(slot):
        parent = PARENTS[0][slot]
        return pltpu.make_async_remote_copy(
            src_ref=idb.at[parent, core], dst_ref=idb.at[slot, core], send_sem=id_s.at[slot], recv_sem=id_r.at[slot],
            device_id=device(minus(OFFSETS[parent], OFFSETS[slot]), 0), device_id_type=MESH)

    def swap_copy(slot):
        return pltpu.make_async_remote_copy(
            src_ref=buf.at[rows_of(slot, 0, ROWS), :], dst_ref=buf.at[rows_of(slot, 0, ROWS), :],
            send_sem=swap_s.at[slot], recv_sem=swap_r.at[slot], device_id=device(ORIGIN, 1), device_id_type=MESH)

    def swap_ids(slot):
        return pltpu.make_async_remote_copy(
            src_ref=idb.at[slot, core], dst_ref=idb.at[slot, core], send_sem=ids_s.at[slot], recv_sem=ids_r.at[slot],
            device_id=device(ORIGIN, 1), device_id_type=MESH)

    def return_copy(slot, flip):
        return pltpu.make_async_remote_copy(
            src_ref=res.at[pl.ds(slot, 1), :], dst_ref=rin.at[pl.ds(slot * 2 + core, 1), :],
            send_sem=ret_s.at[slot, flip], recv_sem=ret_r.at[slot, core],
            device_id=device(OFFSETS[slot], flip), device_id_type=MESH)

    fan = [(slot, flip) for slot in range(SLOTS) for flip in (0, 1) if (slot, flip) != (0, 0)]

    def merge(first, second, count, itself):
        left = pl.ds(pl.multiple_of(first, BLOCK), count)
        right = pl.ds(pl.multiple_of(second * CHIP, CHIP), CHIP)
        top = pl.ds(pl.multiple_of(second * 8, 8), 8)
        scores = lax.dot_general(buf[left, :], buf[right, :], NT, preferred_element_type=jnp.float32)
        mine = idcol[left, :]
        theirs = idrow[pl.ds(pl.multiple_of(second * 8, 8), 1), :]
        best = racc[left, :]
        tops = []
        for tile in range(CHIP // LANES):
            cut = slice(tile * LANES, (tile + 1) * LANES)
            allowed = mine == theirs[:, cut]
            if itself:
                here = lax.broadcasted_iota(jnp.int32, (count, LANES), 0) + first
                there = lax.broadcasted_iota(jnp.int32, (count, LANES), 1) + tile * LANES
                allowed = allowed & (here != there)
            kept = jnp.where(allowed, scores[:, cut], NEG)
            best = jnp.maximum(best, kept)
            if not itself:
                tops.append(jnp.max(kept.reshape(count // 8, 8, LANES), axis=0))
        racc[left, :] = best
        if not itself:
            cacc[top, :] = jnp.maximum(cacc[top, :], jnp.concatenate(tops, axis=1))

    def spread(slot, half):
        tile = idb[slot, half]
        wide = jnp.broadcast_to(tile[:BLOCKS, None, :], (BLOCKS, BLOCK, LANES)).reshape(ROWS, LANES)
        idcol[pl.ds(pl.multiple_of(slot * CHIP + half * ROWS, BLOCK), ROWS), :] = wide

    owner = lax.broadcasted_iota(jnp.int32, (8, LANES), 1) // BLOCK
    sub = lax.broadcasted_iota(jnp.int32, (8, LANES), 0)

    def across(slot):
        both = jnp.concatenate([idb[slot, 0][:BLOCKS], idb[slot, 1][:BLOCKS]], axis=0)
        tiles = [
            jnp.max(jnp.where(owner == sub, both[8 * tile:8 * tile + 8], -1), axis=0, keepdims=True)
            for tile in range(CHIP // LANES)
        ]
        idrow[pl.ds(slot * 8, 8), :] = jnp.broadcast_to(jnp.concatenate(tiles, axis=1), (8, CHIP))

    lanes = lax.broadcasted_iota(jnp.int32, (CHIP, LANES), 1)

    def fold(slots):
        for slot in slots:
            wide = racc[pl.ds(slot * CHIP, CHIP), :]
            mat[...] = jnp.where(lanes == slot, jnp.max(wide, axis=1, keepdims=True), mat[...])

    arrived, here, have = set(), set(), set()

    def arrive(slot, part):
        if slot and (slot, part) not in arrived:
            arrived.add((slot, part))
            data_copy(slot, part).wait_recv()
            if part == 0:
                id_copy(slot).wait_recv()

    def need_half(slot):
        if slot not in here:
            here.add(slot)
            for part in range(PARTS):
                arrive(slot, part)
            spread(slot, core)

    def need(slot):
        need_half(slot)
        if slot not in have:
            have.add(slot)
            swap_copy(slot).wait_recv()
            swap_ids(slot).wait_recv()
            spread(slot, 1 - core)
            across(slot)

    swapped, started = [], False
    for kind, one, part in PROGRAM:
        if kind == SEND:
            arrive(PARENTS[part][one], part)
            if part == 0:
                id_copy(one).start()
            data_copy(one, part).start()
        elif kind == SWAP:
            for index in range(PARTS):
                arrive(one, index)
            swapped.append(one)
            swap_ids(one).start()
            swap_copy(one).start()
        elif kind == FOLD:
            late = {pair[0] for step in STEPS for pair in step if len(pair) == 2}
            fold([slot for slot in range(SLOTS) if slot not in late])
        else:
            if not started:
                started = True
                racc[...] = jnp.full(racc.shape, NEG, jnp.float32)
                cacc[...] = jnp.full(cacc.shape, NEG, jnp.float32)
                mat[...] = jnp.full(mat.shape, NEG, jnp.float32)
                need(0)
                merge(core * ROWS, 0, ROWS, True)
            for pair in STEPS[one]:
                if len(pair) == 2:
                    need_half(pair[0])
                    need(pair[1])
                else:
                    for slot in pair:
                        need(slot)
            for pair in STEPS[one]:
                if len(pair) == 2:
                    merge(pair[0] * CHIP + core * ROWS, pair[1], ROWS, False)
                else:
                    p0, q0, p1, q1 = pair
                    merge((p0 + core * (p1 - p0)) * CHIP, q0 + core * (q1 - q0), CHIP, False)

    fold(sorted(late))
    turned = jnp.transpose(mat[...])[:SLOTS]
    res[...] = jnp.maximum(turned, jnp.max(cacc[...].reshape(SLOTS, 8, CHIP), axis=1))

    for slot, flip in reversed(fan):
        return_copy(slot, flip).start()
    rin[pl.ds(core, 1), :] = res[pl.ds(0, 1), :]

    def wait_return(slot, sender):
        pltpu.make_async_remote_copy(
            src_ref=res.at[pl.ds(slot, 1), :], dst_ref=rin.at[pl.ds(slot * 2 + sender, 1), :],
            send_sem=ret_s.at[slot, 0], recv_sem=ret_r.at[slot, sender],
            device_id=device(ORIGIN, 1), device_id_type=MESH).wait_recv()

    wait_return(0, 1 - core)
    for slot in range(1, SLOTS):
        for sender in (0, 1):
            wait_return(slot, sender)
    joined = jnp.max(rin[...], axis=0, keepdims=True)
    out_ref[...] = jnp.where(core == 0, joined[:, :ROWS], joined[:, ROWS:])

    for slot, flip in fan:
        return_copy(slot, flip).wait_send()
    for slot in swapped:
        swap_ids(slot).wait_send()
        swap_copy(slot).wait_send()
    for slot in range(1, SLOTS):
        id_copy(slot).wait_send()
        for part in range(PARTS):
            data_copy(slot, part).wait_send()


def per_device(embeddings, block_cluster):
    vmem = pl.BlockSpec(memory_space=pltpu.VMEM)
    dma = pltpu.SemaphoreType.DMA
    out = pl.pallas_call(
        kernel,
        out_shape=jax.ShapeDtypeStruct((1, ROWS), jnp.float32),
        in_specs=[pl.BlockSpec(memory_space=pl.ANY)] * 2,
        out_specs=vmem,
        scratch_shapes=[
            pltpu.VMEM((ROWS, WIDTH), jnp.bfloat16),
            pltpu.SMEM((BLOCKS,), jnp.int32),
            pltpu.VMEM((SLOTS * CHIP, WIDTH), jnp.bfloat16),
            pltpu.VMEM((SLOTS, 2, BLOCK, LANES), jnp.int32),
            pltpu.VMEM((SLOTS * CHIP, LANES), jnp.int32),
            pltpu.VMEM((SLOTS * 8, CHIP), jnp.int32),
            pltpu.VMEM((SLOTS * CHIP, LANES), jnp.float32),
            pltpu.VMEM((SLOTS * 8, CHIP), jnp.float32),
            pltpu.VMEM((CHIP, LANES), jnp.float32),
            pltpu.VMEM((SLOTS, CHIP), jnp.float32),
            pltpu.VMEM((SLOTS * 2, CHIP), jnp.float32),
            dma((2,)),
            dma((SLOTS, PARTS)), dma((SLOTS, PARTS)),
            dma((SLOTS,)), dma((SLOTS,)),
            dma((SLOTS,)), dma((SLOTS,)),
            dma((SLOTS,)), dma((SLOTS,)),
            dma((SLOTS, 2)), dma((SLOTS, 2)),
        ],
        compiler_params=pltpu.CompilerParams(
            collective_id=0, has_side_effects=True, vmem_limit_bytes=40 * 2**20),
    )(block_cluster, embeddings)
    return out.reshape(ROWS)


def solution(mesh):
    return jax.shard_map(
        per_device, mesh=mesh, in_specs=(P(("group", "blk"), None), P(("group", "blk"))), out_specs=P(("group", "blk")),
        check_vma=False,
    )
```

time: 70.7 us -> 58.4 us (0.83)
  Pallas kernels: 68.3 us -> 56 us
    pallas_call x1, Pallas kernels: 68.3 us -> 56 us  [per_device(): pl.pallas_call(kernel, out_shape=jax.ShapeDtypeStruct((1, ROWS), jnp.floa...]
where the time goes in v2:
time: 58.4 us; the launch traced here: 58.2 us
  Pallas kernels  56 us (96%)
  local copies, waits for them, and re-layouts  2.21 us (4%)
    pallas_call x1, Pallas kernels, per_device(): pl.pallas_call(kernel, out_shape=jax.ShapeDtypeStruct((1, ROWS), jnp.floa...  56 us
    unnamed x5, local copies, waits for them, and re-layouts  2.21 us

profile of v2, /device:TPU:1, one launch (start us, length us, event | category | flops | bytes accessed | tf_op | source)
XLA Modules:
  0.0 58.2 jit_solution(3332347991720689167)
XLA Ops:
  0.0 0.0 copy-start
  0.0 1.0 %copy-done = bf16[192,1024]{1,0:T(8,128)(2,1)S(1)} copy-done((bf16[192,1024]{1,0:T(8,128)(2,1)S(1)}, bf16[192,1024]{1,0:T(8,128)(2,1)}, u32[]{:S(2)}) %copy-start) | copy-done | bytes 393240
  1.0 0.0 copy-start.1
  1.0 0.7 %copy-done.1 = s32[12]{0:T(128)S(1)} copy-done((s32[12]{0:T(128)S(1)}, s32[12]{0:T(128)}, u32[]{:S(2)}) %copy-start.1) | copy-done | bytes 72
  1.7 56.0 %shard_map.28 = f32[1,192]{1,0:T(1,128)S(1)} custom-call(s32[12]{0:T(128)S(1)} %copy-done.1, bf16[192,1024]{1,0:T(8,128)(2,1)S(1)} %copy-done), custom_call_target="tpu_custom_call" | custom-call | tf_op jit(solution)/shard_map/pallas_call | solution.py:307
  57.7 0.6 copy.4
Async XLA Ops:
  0.0 1.0 %copy-start = (bf16[192,1024]{1,0:T(8,128)(2,1)S(1)}, bf16[192,1024]{1,0:T(8,128)(2,1)}, u32[]{:S(2)}) copy-start(bf16[192,1024]{1,0:T(8,128)(2,1)} %emb_ref.1) | copy-start | bytes 1179652
  1.0 0.7 %copy-start.1 = (s32[12]{0:T(128)S(1)}, s32[12]{0:T(128)}, u32[]{:S(2)}) copy-start(s32[12]{0:T(128)} %ids_ref.1) | copy-start | bytes 148

commit v3 on v2

--- a/solution.py
+++ b/solution.py
@@ -1,3 +1,5 @@
+import functools
+
 import jax
 import jax.numpy as jnp
 from jax import lax
@@ -18,56 +20,49 @@
 
 SEND, SWAP, STEP, FOLD = range(4)
 OFFSETS = (
-    (0, 0, 0), (0, 0, 7), (1, 0, 7), (2, 0, 7), (3, 0, 7), (2, 0, 0), (0, 1, 0), (3, 1, 0),
-    (0, 2, 0), (0, 3, 0), (0, 0, 2), (0, 1, 2), (0, 2, 2), (0, 3, 2), (0, 0, 6), (1, 0, 6),
-    (2, 0, 6),
+    (0, 0, 0), (3, 0, 0), (1, 1, 0), (2, 1, 0), (3, 3, 0), (0, 0, 1), (0, 1, 1), (0, 2, 1),
+    (0, 3, 1), (0, 0, 2), (0, 2, 2), (0, 3, 2), (0, 0, 6), (1, 0, 6), (2, 0, 6), (3, 0, 6),
 )
 PARENTS = (
-    (-1, 0, 1, 2, 3, 3, 0, 6, 6, 0, 0, 12, 13, 10, 15, 16, 3),
-    (-1, 0, 3, 5, 1, 0, 0, 6, 6, 0, 13, 10, 13, 9, 4, 2, 15),
-    (-1, 0, 1, 5, 3, 0, 0, 6, 6, 0, 13, 10, 13, 9, 15, 2, 15),
-    (-1, 0, 1, 2, 1, 3, 0, 6, 9, 0, 0, 10, 13, 10, 1, 2, 3),
+    (-1, 0, 0, 2, 1, 0, 5, 6, 11, 5, 11, 9, 0, 14, 15, 12),
+    (-1, 0, 0, 2, 1, 0, 5, 6, 11, 5, 11, 9, 15, 12, 15, 1),
+    (-1, 0, 0, 2, 0, 0, 5, 8, 0, 5, 7, 8, 0, 12, 13, 12),
 )
 PROGRAM = (
-    (SEND, 1, 0), (SEND, 5, 1), (SEND, 6, 0), (SEND, 9, 0), (SEND, 10, 0), (SWAP, 0, 0), (SEND, 5, 2),
-    (SEND, 1, 3), (SEND, 6, 3), (SEND, 9, 2), (SEND, 1, 2), (SEND, 6, 2), (SEND, 9, 3), (SEND, 10, 3),
-    (SEND, 2, 0), (SEND, 7, 0), (SEND, 6, 1), (SEND, 9, 1), (SEND, 3, 1), (SEND, 2, 3), (SEND, 7, 3),
-    (SEND, 8, 0), (SEND, 3, 2), (SEND, 13, 2), (SEND, 13, 0), (SEND, 2, 2), (SEND, 7, 2), (SEND, 1, 1),
-    (SEND, 8, 2), (SEND, 8, 3), (SEND, 3, 0), (SWAP, 6, 0), (SWAP, 9, 0), (SEND, 7, 1), (SEND, 8, 1),
-    (SEND, 13, 1), (SEND, 15, 3), (SEND, 13, 3), (SEND, 2, 1), (SEND, 3, 3), (SEND, 11, 3), (SEND, 12, 0),
-    (SEND, 15, 2), (SEND, 4, 3), (SEND, 4, 2), (SWAP, 1, 0), (SWAP, 7, 0), (SEND, 10, 2), (SEND, 12, 2),
-    (SEND, 16, 0), (SEND, 5, 0), (SEND, 4, 1), (SEND, 4, 0), (SWAP, 8, 0), (STEP, 0, 0), (SEND, 12, 3),
-    (SWAP, 2, 0), (SEND, 15, 1), (SWAP, 3, 0), (SEND, 5, 3), (STEP, 1, 0), (SEND, 14, 2), (SEND, 16, 2),
-    (SEND, 14, 3), (SEND, 11, 0), (SEND, 10, 1), (SWAP, 13, 0), (STEP, 2, 0), (STEP, 3, 0), (SEND, 15, 0),
-    (SEND, 11, 2), (SEND, 14, 1), (SEND, 12, 1), (SWAP, 4, 0), (STEP, 4, 0), (SEND, 16, 1), (SWAP, 5, 0),
-    (SEND, 16, 3), (STEP, 5, 0), (SEND, 11, 1), (SWAP, 10, 0), (STEP, 6, 0), (STEP, 7, 0), (SEND, 14, 0),
-    (SWAP, 15, 0), (STEP, 8, 0), (SWAP, 12, 0), (STEP, 9, 0), (STEP, 10, 0), (STEP, 11, 0), (STEP, 12, 0),
-    (STEP, 13, 0), (FOLD, 0, 0), (STEP, 14, 0), (STEP, 15, 0), (STEP, 16, 0), (STEP, 17, 0), (STEP, 18, 0),
-    (STEP, 19, 0), (STEP, 20, 0),
+    (SEND, 1, 0), (SEND, 2, 0), (SEND, 5, 0), (SEND, 8, 2), (SEND, 12, 0), (SWAP, 0, 0), (SEND, 4, 2),
+    (SEND, 2, 2), (SEND, 1, 1), (SEND, 2, 1), (SEND, 5, 1), (SEND, 12, 2), (SEND, 4, 0), (SEND, 1, 2),
+    (SEND, 3, 0), (SEND, 6, 0), (SEND, 9, 0), (SEND, 7, 2), (SEND, 15, 0), (SEND, 3, 2), (SEND, 4, 1),
+    (SEND, 6, 1), (SEND, 9, 1), (SEND, 15, 1), (SWAP, 2, 0), (SEND, 3, 1), (SEND, 5, 2), (SWAP, 1, 0),
+    (SEND, 11, 0), (SEND, 7, 0), (SEND, 15, 2), (SEND, 11, 2), (SEND, 13, 2), (SWAP, 4, 0), (SEND, 11, 1),
+    (SEND, 14, 0), (SEND, 7, 1), (STEP, 0, 0), (SWAP, 3, 0), (SWAP, 5, 0), (SEND, 9, 2), (SEND, 6, 2),
+    (SEND, 8, 0), (SEND, 10, 0), (SEND, 12, 1), (SWAP, 15, 0), (SEND, 14, 1), (SEND, 10, 2), (STEP, 1, 0),
+    (SEND, 14, 2), (SWAP, 11, 0), (SEND, 8, 1), (SEND, 10, 1), (SWAP, 7, 0), (SEND, 13, 0), (STEP, 2, 0),
+    (STEP, 3, 0), (STEP, 4, 0), (SWAP, 9, 0), (SWAP, 12, 0), (SEND, 13, 1), (SWAP, 6, 0), (STEP, 5, 0),
+    (STEP, 6, 0), (STEP, 7, 0), (SWAP, 8, 0), (SWAP, 14, 0), (SWAP, 10, 0), (STEP, 8, 0), (STEP, 9, 0),
+    (STEP, 10, 0), (SWAP, 13, 0), (STEP, 11, 0), (STEP, 12, 0), (STEP, 13, 0), (STEP, 14, 0), (STEP, 15, 0),
+    (FOLD, 0, 0), (STEP, 16, 0), (FOLD, 1, 0), (STEP, 17, 0), (FOLD, 2, 0),
 )
 STEPS = (
-    ((6, 0, 6, 9), (1, 0, 1, 6),),
-    ((1, 9, 7, 0), (7, 6, 7, 9),),
-    ((7, 1, 8, 1), (8, 7, 2, 0),),
-    ((2, 9, 2, 8), (3, 0, 3, 1),),
-    ((3, 6, 3, 9), (3, 7, 3, 8),),
-    ((13, 0, 13, 1), (13, 6, 13, 7),),
-    ((13, 8, 13, 9), (13, 2, 13, 3),),
-    ((4, 0, 4, 8), (4, 9, 4, 13),),
-    ((5, 6, 5, 8), (5, 13, 10, 1),),
-    ((10, 2, 10, 3), (10, 7, 10, 4),),
-    ((10, 5, 15, 0), (15, 5, 15, 6),),
-    ((15, 7, 15, 8), (15, 9, 15, 13),),
-    ((15, 10, 12, 1), (12, 2, 12, 3),),
-    ((12, 4, 12, 5),),
-    ((12, 7), (12, 15),),
-    ((11, 1), (11, 2),),
-    ((11, 3), (11, 4),),
-    ((11, 15), (16, 10),),
-    ((16, 13), (16, 12),),
-    ((14, 10), (14, 12),),
-    ((14, 13),),
+    ((2, (0, 1)), (4, (1, 2))),
+    ((3, (1, 4)), (5, (3, 4))),
+    ((15, (1, 4)), (15, (0, 3))),
+    ((15, (2, 5)), (5, (2, 0))),
+    ((11, (5, 1)), (11, (2, 3))),
+    ((11, (15, 7)), (7, (0, 1))),
+    ((7, (4, 2)), (7, (3, 5))),
+    ((15, (7, 9)), (9, (3, 2))),
+    ((12, (7, 11)), (6, (3, 15))),
+    ((9, (4, 12)), (12, (1, 5))),
+    ((8, (3, 15)), (6, (2, 12))),
+    ((14, (0, 3)), (14, (5, 6))),
+    ((14, (7, 8)), (14, (9, 11))),
+    ((12, (14, 10)), (10, (0, 1))),
+    ((10, (15, 14)), (13, (5, 6))),
+    ((13, (7, 8)), (8, (2, 12))),
+    ((13, (11,)), (1, (0,))),
+    ((5, (1,)),),
 )
+FOLDS = ((10, 14, 3, 7, 15, 2, 4, 6, 8, 9, 12), (11, 13, 0), (1, 5))
 
 SLOTS = len(OFFSETS)
 PARTS = len(PARENTS)
@@ -157,31 +152,34 @@
             send_sem=ret_s.at[slot, flip], recv_sem=ret_r.at[slot, core],
             device_id=device(OFFSETS[slot], flip), device_id_type=MESH)
 
-    fan = [(slot, flip) for slot in range(SLOTS) for flip in (0, 1) if (slot, flip) != (0, 0)]
-
-    def merge(first, second, count, itself):
+    used = sorted(slot for group in FOLDS for slot in group)
+    fan = [(slot, flip) for slot in used for flip in (0, 1) if (slot, flip) != (0, 0)]
+
+    def merge(first, seconds, count, itself):
         left = pl.ds(pl.multiple_of(first, BLOCK), count)
-        right = pl.ds(pl.multiple_of(second * CHIP, CHIP), CHIP)
-        top = pl.ds(pl.multiple_of(second * 8, 8), 8)
-        scores = lax.dot_general(buf[left, :], buf[right, :], NT, preferred_element_type=jnp.float32)
+        others = [buf[pl.ds(pl.multiple_of(one * CHIP, CHIP), CHIP), :] for one in seconds]
+        right = jnp.concatenate(others, axis=0) if len(others) > 1 else others[0]
+        scores = lax.dot_general(buf[left, :], right, NT, preferred_element_type=jnp.float32)
         mine = idcol[left, :]
-        theirs = idrow[pl.ds(pl.multiple_of(second * 8, 8), 1), :]
         best = racc[left, :]
-        tops = []
-        for tile in range(CHIP // LANES):
-            cut = slice(tile * LANES, (tile + 1) * LANES)
-            allowed = mine == theirs[:, cut]
-            if itself:
-                here = lax.broadcasted_iota(jnp.int32, (count, LANES), 0) + first
-                there = lax.broadcasted_iota(jnp.int32, (count, LANES), 1) + tile * LANES
-                allowed = allowed & (here != there)
-            kept = jnp.where(allowed, scores[:, cut], NEG)
-            best = jnp.maximum(best, kept)
+        for index, one in enumerate(seconds):
+            top = pl.ds(pl.multiple_of(one * 8, 8), 8)
+            theirs = idrow[pl.ds(pl.multiple_of(one * 8, 8), 1), :]
+            tops = []
+            for tile in range(CHIP // LANES):
+                at = index * CHIP + tile * LANES
+                allowed = mine == theirs[:, tile * LANES:(tile + 1) * LANES]
+                if itself:
+                    here = lax.broadcasted_iota(jnp.int32, (count, LANES), 0) + first
+                    there = lax.broadcasted_iota(jnp.int32, (count, LANES), 1) + at
+                    allowed = allowed & (here != there)
+                kept = jnp.where(allowed, scores[:, at:at + LANES], NEG)
+                best = jnp.maximum(best, kept)
+                if not itself:
+                    tops.append(jnp.max(kept.reshape(count // 8, 8, LANES), axis=0))
             if not itself:
-                tops.append(jnp.max(kept.reshape(count // 8, 8, LANES), axis=0))
+                cacc[top, :] = jnp.maximum(cacc[top, :], jnp.concatenate(tops, axis=1))
         racc[left, :] = best
-        if not itself:
-            cacc[top, :] = jnp.maximum(cacc[top, :], jnp.concatenate(tops, axis=1))
 
     def spread(slot, half):
         tile = idb[slot, half]
@@ -205,6 +203,14 @@
         for slot in slots:
             wide = racc[pl.ds(slot * CHIP, CHIP), :]
             mat[...] = jnp.where(lanes == slot, jnp.max(wide, axis=1, keepdims=True), mat[...])
+        turned = jnp.transpose(mat[...])
+        for slot in slots:
+            tops = jnp.max(cacc[pl.ds(slot * 8, 8), :], axis=0, keepdims=True)
+            res[pl.ds(slot, 1), :] = jnp.maximum(turned[slot:slot + 1], tops)
+        for slot in slots:
+            for flip in (0, 1):
+                if (slot, flip) != (0, 0):
+                    return_copy(slot, flip).start()
 
     arrived, here, have = set(), set(), set()
 
@@ -245,8 +251,7 @@
             swap_ids(one).start()
             swap_copy(one).start()
         elif kind == FOLD:
-            late = {pair[0] for step in STEPS for pair in step if len(pair) == 2}
-            fold([slot for slot in range(SLOTS) if slot not in late])
+            fold(FOLDS[one])
         else:
             if not started:
                 started = True
@@ -254,27 +259,19 @@
                 cacc[...] = jnp.full(cacc.shape, NEG, jnp.float32)
                 mat[...] = jnp.full(mat.shape, NEG, jnp.float32)
                 need(0)
-                merge(core * ROWS, 0, ROWS, True)
-            for pair in STEPS[one]:
-                if len(pair) == 2:
-                    need_half(pair[0])
-                    need(pair[1])
-                else:
-                    for slot in pair:
-                        need(slot)
-            for pair in STEPS[one]:
-                if len(pair) == 2:
-                    merge(pair[0] * CHIP + core * ROWS, pair[1], ROWS, False)
-                else:
-                    p0, q0, p1, q1 = pair
-                    merge((p0 + core * (p1 - p0)) * CHIP, q0 + core * (q1 - q0), CHIP, False)
-
-    fold(sorted(late))
-    turned = jnp.transpose(mat[...])[:SLOTS]
-    res[...] = jnp.maximum(turned, jnp.max(cacc[...].reshape(SLOTS, 8, CHIP), axis=1))
-
-    for slot, flip in reversed(fan):
-        return_copy(slot, flip).start()
+                merge(core * ROWS, [0], ROWS, True)
+            if len(STEPS[one]) == 1:
+                (first, seconds), = STEPS[one]
+                need_half(first)
+                for slot in seconds:
+                    need(slot)
+                merge(first * CHIP + core * ROWS, seconds, ROWS, False)
+            else:
+                (p0, q0), (p1, q1) = STEPS[one]
+                for slot in (p0, p1, *q0, *q1):
+                    need(slot)
+                merge((p0 + core * (p1 - p0)) * CHIP, [a + core * (b - a) for a, b in zip(q0, q1)], CHIP, False)
+
     rin[pl.ds(core, 1), :] = res[pl.ds(0, 1), :]
 
     def wait_return(slot, sender):
@@ -284,10 +281,12 @@
             device_id=device(ORIGIN, 1), device_id_type=MESH).wait_recv()
 
     wait_return(0, 1 - core)
-    for slot in range(1, SLOTS):
+    for slot in used:
         for sender in (0, 1):
-            wait_return(slot, sender)
-    joined = jnp.max(rin[...], axis=0, keepdims=True)
+            if slot:
+                wait_return(slot, sender)
+    joined = functools.reduce(jnp.maximum, [rin[pl.ds(2 * slot, 2), :] for slot in used])
+    joined = jnp.max(joined, axis=0, keepdims=True)
     out_ref[...] = jnp.where(core == 0, joined[:, :ROWS], joined[:, ROWS:])
 
     for slot, flip in fan:
@@ -307,7 +306,7 @@
     out = pl.pallas_call(
         kernel,
         out_shape=jax.ShapeDtypeStruct((1, ROWS), jnp.float32),
-        in_specs=[pl.BlockSpec(memory_space=pl.ANY)] * 2,
+        in_specs=[pl.BlockSpec(memory_space=pltpu.HBM)] * 2,
         out_specs=vmem,
         scratch_shapes=[
             pltpu.VMEM((ROWS, WIDTH), jnp.bfloat16),

time: 58.4 us -> 57.3 us (0.981)
  Pallas kernels: 56 us -> 54.9 us
    pallas_call x1, Pallas kernels: 56 us -> 54.9 us  [per_device(): pl.pallas_call(kernel, out_shape=jax.ShapeDtypeStruct((1, ROWS), jnp.floa...]
where the time goes in v3:
time: 57.3 us; the launch traced here: 57.1 us
  Pallas kernels  54.9 us (96%)
  local copies, waits for them, and re-layouts  2.21 us (4%)
    pallas_call x1, Pallas kernels, per_device(): pl.pallas_call(kernel, out_shape=jax.ShapeDtypeStruct((1, ROWS), jnp.floa...  54.9 us
    unnamed x5, local copies, waits for them, and re-layouts  2.21 us

profile of v3, /device:TPU:1, one launch (start us, length us, event | category | flops | bytes accessed | tf_op | source)
XLA Modules:
  0.0 57.1 jit_solution(4069078029532064512)
XLA Ops:
  0.0 0.0 copy-start
  0.0 1.0 %copy-done = bf16[192,1024]{1,0:T(8,128)(2,1)S(1)} copy-done((bf16[192,1024]{1,0:T(8,128)(2,1)S(1)}, bf16[192,1024]{1,0:T(8,128)(2,1)}, u32[]{:S(2)}) %copy-start) | copy-done | bytes 393240
  1.0 0.0 copy-start.1
  1.0 0.7 %copy-done.1 = s32[12]{0:T(128)S(1)} copy-done((s32[12]{0:T(128)S(1)}, s32[12]{0:T(128)}, u32[]{:S(2)}) %copy-start.1) | copy-done | bytes 72
  1.7 54.9 %shard_map.28 = f32[1,192]{1,0:T(1,128)S(1)} custom-call(s32[12]{0:T(128)S(1)} %copy-done.1, bf16[192,1024]{1,0:T(8,128)(2,1)S(1)} %copy-done), custom_call_target="tpu_custom_call" | custom-call | tf_op jit(solution)/shard_map/pallas_call | solution.py:306
  56.6 0.6 copy.4
Async XLA Ops:
  0.0 1.0 %copy-start = (bf16[192,1024]{1,0:T(8,128)(2,1)S(1)}, bf16[192,1024]{1,0:T(8,128)(2,1)}, u32[]{:S(2)}) copy-start(bf16[192,1024]{1,0:T(8,128)(2,1)} %emb_ref.1) | copy-start | bytes 1179652
  1.0 0.7 %copy-start.1 = (s32[12]{0:T(128)S(1)}, s32[12]{0:T(128)}, u32[]{:S(2)}) copy-start(s32[12]{0:T(128)} %ids_ref.1) | copy-start | bytes 148

commit v4 on v3

--- a/solution.py
+++ b/solution.py
@@ -133,7 +133,7 @@
     def id_copy(slot):
         parent = PARENTS[0][slot]
         return pltpu.make_async_remote_copy(
-            src_ref=idb.at[parent, core], dst_ref=idb.at[slot, core], send_sem=id_s.at[slot], recv_sem=id_r.at[slot],
+            src_ref=idb.at[parent], dst_ref=idb.at[slot], send_sem=id_s.at[slot], recv_sem=id_r.at[slot],
             device_id=device(minus(OFFSETS[parent], OFFSETS[slot]), 0), device_id_type=MESH)
 
     def swap_copy(slot):
@@ -233,22 +233,28 @@
         if slot not in have:
             have.add(slot)
             swap_copy(slot).wait_recv()
-            swap_ids(slot).wait_recv()
             spread(slot, 1 - core)
             across(slot)
 
-    swapped, started = [], False
+    swapped, started, paired, waiting = [], False, False, []
+    swap_ids(0).start()
     for kind, one, part in PROGRAM:
+        if not paired and (kind != SEND or PARENTS[part][one]):
+            paired = True
+            swap_ids(0).wait_recv()
+            for slot in waiting:
+                id_copy(slot).start()
         if kind == SEND:
             arrive(PARENTS[part][one], part)
-            if part == 0:
+            if part == 0 and paired:
                 id_copy(one).start()
+            elif part == 0:
+                waiting.append(one)
             data_copy(one, part).start()
         elif kind == SWAP:
             for index in range(PARTS):
                 arrive(one, index)
             swapped.append(one)
-            swap_ids(one).start()
             swap_copy(one).start()
         elif kind == FOLD:
             fold(FOLDS[one])
@@ -291,8 +297,8 @@
 
     for slot, flip in fan:
         return_copy(slot, flip).wait_send()
+    swap_ids(0).wait_send()
     for slot in swapped:
-        swap_ids(slot).wait_send()
         swap_copy(slot).wait_send()
     for slot in range(1, SLOTS):
         id_copy(slot).wait_send()

time: 57.3 us -> 57.7 us (level)
  no operation moved by 1% of the time
where the time goes in v4:
time: 57.7 us; the launch traced here: 57.6 us
  Pallas kernels  55.4 us (96%)
  local copies, waits for them, and re-layouts  2.21 us (4%)
    pallas_call x1, Pallas kernels, per_device(): pl.pallas_call(kernel, out_shape=jax.ShapeDtypeStruct((1, ROWS), jnp.floa...  55.4 us
    unnamed x5, local copies, waits for them, and re-layouts  2.21 us

profile of v4, /device:TPU:1, one launch (start us, length us, event | category | flops | bytes accessed | tf_op | source)
XLA Modules:
  0.0 57.6 jit_solution(7382475748050392120)
XLA Ops:
  0.0 0.0 copy-start
  0.0 1.0 %copy-done = bf16[192,1024]{1,0:T(8,128)(2,1)S(1)} copy-done((bf16[192,1024]{1,0:T(8,128)(2,1)S(1)}, bf16[192,1024]{1,0:T(8,128)(2,1)}, u32[]{:S(2)}) %copy-start) | copy-done | bytes 393240
  1.0 0.0 copy-start.1
  1.0 0.7 %copy-done.1 = s32[12]{0:T(128)S(1)} copy-done((s32[12]{0:T(128)S(1)}, s32[12]{0:T(128)}, u32[]{:S(2)}) %copy-start.1) | copy-done | bytes 72
  1.7 55.4 %shard_map.28 = f32[1,192]{1,0:T(1,128)S(1)} custom-call(s32[12]{0:T(128)S(1)} %copy-done.1, bf16[192,1024]{1,0:T(8,128)(2,1)S(1)} %copy-done), custom_call_target="tpu_custom_call" | custom-call | tf_op jit(solution)/shard_map/pallas_call | solution.py:312
  57.1 0.6 copy.4
Async XLA Ops:
  0.0 1.0 %copy-start = (bf16[192,1024]{1,0:T(8,128)(2,1)S(1)}, bf16[192,1024]{1,0:T(8,128)(2,1)}, u32[]{:S(2)}) copy-start(bf16[192,1024]{1,0:T(8,128)(2,1)} %emb_ref.1) | copy-start | bytes 1179652
  1.0 0.7 %copy-start.1 = (s32[12]{0:T(128)S(1)}, s32[12]{0:T(128)}, u32[]{:S(2)}) copy-start(s32[12]{0:T(128)} %ids_ref.1) | copy-start | bytes 148
